TPU v7x, 256 devices: a whole 4x4x8 slice. The times are simulated.
256 devices in a mesh: tok: 4 (over z_hi, core), col: 64 (over y, x, z_lo).
Axes of the slice: x: 4, y: 4, z: 8 (z_hi: 2, z_lo: 4; z = z_hi * 4 + z_lo), core: 2. Of those that a mesh axis runs over, the one named last changes fastest.
Arguments:
- acts_t: bfloat16 [4096, 2048], P('col', 'tok'), may hold values from -6 to 6
- grads_t: bfloat16 [14336, 2048], P('col', 'tok'), may hold values from -6 to 6
- basis_a: bfloat16 [4096, 4096], P('col'), may hold values from -0.09375 to 0.09375
- basis_g: bfloat16 [14336, 14336], P('col'), may hold values from -0.046875 to 0.046875
Outputs:
- scaling: float32 [14336, 4096], P('col', 'tok')
All inputs are finite; a program needn't handle non-finite values.
Results may differ from a plain program's by a relative error of at most 0.0003.
Values may be sent and summed in bfloat16 or wider, within the bound.
A program may use at most 128 MiB of HBM per device.

v0:
```python
import jax
import jax.numpy as jnp
from jax import lax
from jax.sharding import PartitionSpec as P


def project_with(basis, piece):
    return jnp.dot(basis, piece, preferred_element_type=jnp.float32)


def body(acts_t, grads_t, basis_a, basis_g):
    tok_cols = acts_t.shape[1]
    tok_groups = lax.axis_size("tok")
    total_cols = tok_cols * tok_groups
    proj_a = project_with(basis_a, lax.all_gather(acts_t, "col", axis=0, tiled=True))
    sq_a = (proj_a * proj_a).astype(jnp.bfloat16)
    proj_g = project_with(basis_g, lax.all_gather(grads_t, "col", axis=0, tiled=True))
    sq_g = (proj_g * proj_g).astype(jnp.bfloat16)
    sq_full = lax.all_gather(sq_a, "col", axis=0, tiled=True)
    partial_tile = lax.dot_general(
        sq_g, sq_full, (((1,), (1,)), ((), ())), preferred_element_type=jnp.float32
    )
    summed = lax.psum_scatter(partial_tile, "tok", scatter_dimension=1, tiled=True)
    return summed / jnp.float32(total_cols)


def solution(mesh):
    return jax.shard_map(
        body,
        mesh=mesh,
        in_specs=(P("col", "tok"), P("col", "tok"), P("col", None), P("col", None)),
        out_specs=P("col", "tok"),
        check_vma=False,
    )
```

profile of v0, /device:TPU:1, one launch (start us, length us, event | category | flops | bytes accessed | tf_op | source)
XLA Modules:
  0.0 1231.1 jit_solution(13431609149992799794)
XLA Ops:
  6.5 0.0 copy-start
  6.5 0.0 all-gather.6.cloned.1.call-start
  6.5 0.7 all-gather.6.cloned.1.call-update
  7.3 0.0 all-gather.8.cloned.1.call-start
  7.3 323.4 %all-gather.6.cloned.1.call-done = bf16[4096,512]{1,0:T(8,128)(2,1)} async-done(((bf16[64,512]{1,0:T(8,128)(2,1)}), bf16[4096,512]{1,0:T(8,128)(2,1)}) %all-gather.6.cloned.1.call-update) | async-done | bytes 4194320 | tf_op jit(solution)/shard_map/all_gather | solution.py:15
  330.7 0.0 copy-done
  330.7 3.7 fusion.1
  334.3 0.0 all-gather.8.cloned.1.call-update
  334.4 0.0 all-gather.4.cloned.1.call-start
  334.4 0.7 all-gather.4.cloned.1.call-update
  335.1 0.0 reduce-scatter.2.cloned.1.call-start
  335.1 355.4 %all-gather.8.cloned.1.call-done = bf16[4096,512]{1,0:T(8,128)(2,1)} async-done(((bf16[64,512]{1,0:T(8,128)(2,1)}), bf16[4096,512]{1,0:T(8,128)(2,1)}) %all-gather.8.cloned.1.call-update) | async-done | bytes 4194320 | tf_op jit(solution)/shard_map/all_gather | solution.py:19
  690.6 405.8 %all-gather.4.cloned.1.call-done = bf16[14336,512]{1,0:T(8,128)(2,1)} async-done(((bf16[224,512]{1,0:T(8,128)(2,1)}), bf16[14336,512]{1,0:T(8,128)(2,1)}) %all-gather.4.cloned.1.call-update) | async-done | bytes 14680080 | tf_op jit(solution)/shard_map/all_gather | solution.py:17
  1096.3 14.8 %fusion.2 = f32[224,4096]{1,0:T(8,128)} fusion(bf16[4096,512]{1,0:T(8,128)(2,1)} %all-gather.8.cloned.1.call-done, bf16[224,14336]{1,0:T(8,128)(2,1)} %param.7, bf16[14336,512]{1,0:T(8,128)(2,1)} %all-gather.4.cloned.1.call-done), kind=kOutput, calls=%fused_computation.4 | convolution fusion | flops 4228087808 | bytes 28966912 | tf_op jit(solution)/shard_map/dot_general | solution.py:20
  1111.1 0.0 reduce-scatter.2.cloned.1.call-update
  1111.2 111.2 %reduce-scatter.2.cloned.1.call-done = f32[224,1024]{1,0:T(8,128)} async-done(((f32[224,4096]{1,0:T(8,128)}), f32[224,1024]{1,0:T(8,128)}) %reduce-scatter.2.cloned.1.call-update) | async-done | bytes 917520 | tf_op jit(solution)/shard_map/reduce_scatter | solution.py:23
  1222.4 2.2 broadcast_multiply_fusion
Async XLA Ops:
  6.5 324.1 %copy-start = (bf16[64,4096]{1,0:T(8,128)(2,1)S(1)}, bf16[64,4096]{1,0:T(8,128)(2,1)}, u32[]{:S(2)}) copy-start(bf16[64,4096]{1,0:T(8,128)(2,1)} %param.6) | copy-start | bytes 1572868
  6.5 324.1 %all-gather.6.cloned.1.call-start = ((), (), s32[]{:S(2)}) async-start(), calls=%async_computation.2 | async-start | bytes 4259840 | tf_op jit(solution)/shard_map/all_gather | solution.py:15
  7.3 683.3 %all-gather.8.cloned.1.call-start = ((), (), s32[]{:S(2)}) async-start(), calls=%async_computation.3 | async-start | bytes 4259840 | tf_op jit(solution)/shard_map/all_gather | solution.py:19
  334.4 762.0 %all-gather.4.cloned.1.call-start = ((), (), s32[]{:S(2)}) async-start(), calls=%async_computation.1 | async-start | bytes 14909440 | tf_op jit(solution)/shard_map/all_gather | solution.py:17
  335.1 887.3 %reduce-scatter.2.cloned.1.call-start = ((), (), s32[]{:S(2)}) async-start(), calls=%async_computation.4 | async-start | bytes 4587520 | tf_op jit(solution)/shard_map/reduce_scatter | solution.py:23
Sparse Core Ops, SparseCore 0:
  9.1 321.4 all-gather.5
  334.5 356.0 all-gather.7
  692.3 403.9 all-gather.3
  1111.3 111.0 reduce-scatter.1
where the time goes:
time: 1230 us
  waiting for transfers between devices  1200 us (98%)
  matrix products  18.5 us (2%)
  between operations  13.1 us (1%)
    all_gather x1, waiting for transfers between devices, body(): lax.all_gather(grads_t, 'col', axis=0, tiled=True)  406 us
    all_gather x1, waiting for transfers between devices, body(): sq_full = lax.all_gather(sq_a, 'col', axis=0, tiled=True)  355 us
    all_gather x1, waiting for transfers between devices, body(): lax.all_gather(acts_t, 'col', axis=0, tiled=True)  323 us
    reduce_scatter x1, waiting for transfers between devices, body(): lax.psum_scatter(partial_tile, 'tok', scatter_dimension=1, tiled=True)  111 us
  transfers between devices with their start and end apart: 4, of which 4 were waited for; matrix products, arithmetic and copies ran while one was open for 0% of the time, Pallas kernels for 0%

commit v1 on v0

v1 whole, which is shorter than its diff:
```python
import jax
import jax.numpy as jnp
from jax import lax
from jax.experimental import pallas as pl
from jax.experimental.pallas import tpu as pltpu
from jax.sharding import PartitionSpec as P

MESH = pl.DeviceIdType.MESH
BF16 = jnp.bfloat16
F32 = jnp.float32
NX, NY, NZ, NT = 4, 4, 4, 4


class Sems:
    def __init__(self, send, recv):
        self.send, self.recv, self.used = send, recv, 0

    def take(self):
        i = self.used
        self.used += 1
        return self.send.at[i], self.recv.at[i]


N_COPIES = 104
N_LOCAL = 12


def kernel(acts, grads, basis_a, basis_g, out, xa, ba, pa, ra, sa, sq, xg, bg, acc, ps, pr, sg,
           send_sem, recv_sem, local_sem):
    tok = lax.axis_index("tok")
    col = lax.axis_index("col")
    zl = lax.rem(col, 4)
    x = lax.rem(lax.div(col, 4), 4)
    y = lax.div(col, 16)
    c = lax.rem(tok, 2)
    da, fa = acts.shape[0], basis_a.shape[1] // NY
    dg = grads.shape[0]
    half = dg // 2
    fx = NZ * dg
    fy = NX * fx
    cols = acts.shape[1]
    quarter = cols // NY

    def up(v, d):
        return lax.rem(v + d, 4)

    def dn(v, d):
        return lax.rem(v + 4 - d, 4)

    def dev(tok=tok, y=y, x=x, zl=zl):
        return (tok, (y * 4 + x) * 4 + zl)

    sib = tok + 1 - 2 * c
    far = up(tok, 2)

    barrier = pltpu.get_barrier_semaphore()
    partners = [dev(tok=up(tok, dt), zl=up(zl, dz)) for dt in range(4) for dz in range(4) if dt or dz]
    partners += [dev(x=up(x, d)) for d in (1, 2, 3)] + [dev(y=up(y, d)) for d in (1, 2, 3)]
    for p in partners:
        pl.semaphore_signal(barrier, inc=1, device_id=p, device_id_type=MESH)
    pl.semaphore_wait(barrier, len(partners))

    sems = Sems(send_sem, recv_sem)
    sent = []

    class Copy:
        def __init__(self, tag, landing):
            self.tag, self.landing, self.sems = tag, landing, sems.take()

        def start(self, src, dst, to):
            s, r = self.sems
            cp = pltpu.make_async_remote_copy(src_ref=src, dst_ref=dst, send_sem=s, recv_sem=r,
                                              device_id=to, device_id_type=MESH)
            cp.start()
            sent.append(cp)

        def arrived(self):
            s, r = self.sems
            pltpu.make_async_remote_copy(src_ref=self.landing, dst_ref=self.landing, send_sem=s, recv_sem=r,
                                         device_id=dev(), device_id_type=MESH).wait_recv()

    n_local = [0]

    def local(src, dst):
        cp = pltpu.make_async_copy(src, dst, local_sem.at[n_local[0]])
        n_local[0] += 1
        cp.start()
        return cp

    def xa_at(xs, zs):
        return xa.at[pl.ds(pl.multiple_of(xs * (NZ * da) + zs * da, da), da), :]

    def ba_at(ys):
        return ba.at[pl.ds(pl.multiple_of(ys * da, da), da), :]

    def ba_cols(ys):
        return basis_a.at[:, pl.ds(pl.multiple_of(ys * fa, fa), fa)]

    def xg_at(ys, zs):
        return xg.at[ys, pl.ds(pl.multiple_of(zs * dg, 32), dg), :]

    def bg_at(h, ys, xs):
        return bg.at[h, ys, pl.ds(pl.multiple_of(xs * half, 16), half), :]

    def bg_cols(h, ys, xs):
        return basis_g.at[h * half:(h + 1) * half, pl.ds(pl.multiple_of(ys * fy + xs * fx, 128), fx)]

    def sq_block(t, xs, zs, q):
        return sq.at[t, pl.ds(pl.multiple_of((xs * NZ + zs) * da, da), da), pl.ds(pl.multiple_of(q * quarter, quarter), quarter)]

    def sq_chunk(xs, q):
        return sq.at[:, pl.ds(pl.multiple_of(xs * (NZ * da), NZ * da), NZ * da), pl.ds(pl.multiple_of(q * quarter, quarter), quarter)]

    three = (1, 3, 2)

    a_z = {d: Copy("a_z", xa_at(x, dn(zl, d))) for d in three}
    a_x = {(j, d): Copy("a_x", xa_at(dn(x, d), dn(zl, j))) for j in range(4) for d in three}
    b_a = {d: Copy("b_a", ba_at(dn(y, d))) for d in three}
    g_z = {d: Copy("g_z", xg_at(y, dn(zl, d))) for d in three}
    g_y = {(j, d): Copy("g_y", xg_at(dn(y, d), dn(zl, j))) for j in range(4) for d in (1, 3)}
    g_f = {j: Copy("g_f", xg_at(up(y, 2), dn(zl, j))) for j in range(4)}
    mine = [up(y, 3 * c), up(y, 1 + c)]
    theirs = [up(y, 3 * (1 - c)), up(y, 2 - c)]
    b_x = {(h, k, d): Copy("b_x", bg_at(h, mine[k], dn(x, d))) for h in range(2) for k in range(2) for d in three}
    b_s = {(h, k, d): Copy("b_s", bg_at(h, theirs[k], dn(x, d))) for h in range(2) for k in range(2) for d in three}

    def send_grads_z(d):
        g_z[d].start(grads, xg_at(y, zl), dev(zl=up(zl, d)))

    def send_basis(h, k, d):
        b_x[h, k, d].start(bg_cols(h, mine[k], up(x, d)), bg_at(h, mine[k], x), dev(x=up(x, d)))

    def share_basis(h, k):
        for d in three:
            b_x[h, k, d].arrived()
            b_s[h, k, d].start(bg_at(h, mine[k], dn(x, d)), bg_at(h, mine[k], dn(x, d)), dev(tok=sib))

    def spread_grads(j):
        g_z[j].arrived()
        for d in (1, 3):
            g_y[j, d].start(xg_at(y, dn(zl, j)), xg_at(y, dn(zl, j)), dev(y=up(y, d)))

    def forward_grads(j):
        d = 1 if j < 2 else 3
        g_y[j, d].arrived()
        g_f[j].start(xg_at(dn(y, d), dn(zl, j)), xg_at(dn(y, d), dn(zl, j)), dev(y=up(y, d)))

    for d in three:
        a_z[d].start(acts, xa_at(x, zl), dev(zl=up(zl, d)))
    for d in three:
        a_x[0, d].start(acts, xa_at(x, zl), dev(x=up(x, d)))
    for d in three:
        b_a[d].start(ba_cols(up(y, d)), ba_at(y), dev(y=up(y, d)))
    send_grads_z(1)
    for d in (1, 3):
        g_y[0, d].start(grads, xg_at(y, zl), dev(y=up(y, d)))
    for d in (1, 3):
        send_basis(0, 0, d)
    a_own = local(acts, xa_at(x, zl))
    ba_own = local(ba_cols(y), ba_at(y))
    g_own = local(grads, xg_at(y, zl))
    bg_own = [local(bg_cols(h, ys, x), bg_at(h, ys, x)) for h in range(2) for ys in mine + theirs]

    for j in three:
        a_z[j].arrived()
        for d in three:
            a_x[j, d].start(xa_at(x, dn(zl, j)), xa_at(x, dn(zl, j)), dev(x=up(x, d)))
    send_grads_z(3)
    send_grads_z(2)
    send_basis(0, 0, 2)
    for d in three:
        send_basis(0, 1, d)
    spread_grads(1)
    forward_grads(0)

    a_own.wait()
    ba_own.wait()
    for d in three:
        b_a[d].arrived()
    for key in a_x:
        a_x[key].arrived()
    for ys in range(NY):
        pa[ys] = jnp.dot(ba[...], xa[:, ys * quarter:(ys + 1) * quarter], preferred_element_type=F32)
    p_a = {d: Copy("p_a", ra.at[d - 1]) for d in three}
    for d in three:
        p_a[d].start(pa.at[up(y, d)], ra.at[d - 1], dev(y=up(y, d)))
    spread_grads(3)
    forward_grads(1)
    share_basis(0, 0)
    for d in three:
        p_a[d].arrived()
    total_a = pa[y] + ra[0] + ra[1] + ra[2]
    sa[...] = (total_a * total_a).astype(BF16)

    s_z = {(dt, dz): Copy("s_z", sq_block(dn(tok, dt), x, dn(zl, dz), y)) for dt in range(4) for dz in range(4) if dt or dz}
    for dt, dz in s_z:
        t = up(tok, dt)
        s_z[dt, dz].start(sa.at[pl.ds(pl.multiple_of(t * da, da), da), :], sq_block(tok, x, zl, y),
                          dev(tok=t, zl=up(zl, dz)))
    s_own = local(sa.at[pl.ds(pl.multiple_of(tok * da, da), da), :], sq_block(tok, x, zl, y))
    s_x = {d: Copy("s_x", sq_chunk(dn(x, d), y)) for d in three}
    s_y = {(j, d): Copy("s_y", sq_chunk(dn(x, j), dn(y, d))) for j in range(4) for d in (1, 3)}
    s_f = {j: Copy("s_f", sq_chunk(dn(x, j), up(y, 2))) for j in range(4)}

    def spread_sq(j):
        for d in (1, 3):
            s_y[j, d].start(sq_chunk(dn(x, j), y), sq_chunk(dn(x, j), y), dev(y=up(y, d)))

    def forward_sq(j):
        d = 1 if j < 2 else 3
        s_y[j, d].arrived()
        s_f[j].start(sq_chunk(dn(x, j), dn(y, d)), sq_chunk(dn(x, j), dn(y, d)), dev(y=up(y, d)))

    spread_grads(2)
    for d in three:
        send_basis(1, 0, d)
    s_own.wait()
    for key in s_z:
        s_z[key].arrived()
    for d in three:
        s_x[d].start(sq_chunk(x, y), sq_chunk(x, y), dev(x=up(x, d)))
    spread_sq(0)
    share_basis(0, 1)
    for d in three:
        send_basis(1, 1, d)
    forward_grads(3)
    forward_grads(2)

    g_own.wait()
    for cp in bg_own:
        cp.wait()

    def basis_there(h, k):
        for d in three:
            b_s[h, k, d].arrived()

    def add_range(h, ys, first=False):
        part = jnp.dot(bg[h, ys], xg[ys], preferred_element_type=F32)
        acc[h] = part if first else acc[h] + part

    p_g = {(h, d): Copy("p_g", pr.at[h, d - 1]) for h in range(2) for d in three}

    def exchange_products(h):
        ps[h] = acc[h].astype(BF16)
        for d in (2, 1, 3):
            xs = up(x, d)
            p_g[h, d].start(ps.at[h, pl.ds(pl.multiple_of(xs * half, 16), half), :], pr.at[h, d - 1], dev(x=xs))

    def sg_at(t, h):
        return sg.at[t, h * half:(h + 1) * half, :]

    t_far = [Copy("t_far", sg_at(far, h)) for h in range(2)]
    t_sib = [Copy("t_sib", sg_at(sib, h)) for h in range(2)]
    t_both = [Copy("t_both", sg_at(up(sib, 2), h)) for h in range(2)]

    def square_products(h):
        for d in three:
            p_g[h, d].arrived()
        own = acc[h, pl.ds(pl.multiple_of(x * half, 8), half), :]
        total = own + pr[h, 0].astype(F32) + pr[h, 1].astype(F32) + pr[h, 2].astype(F32)
        sg[tok, h * half:(h + 1) * half, :] = (total * total).astype(BF16)
        t_far[h].start(sg_at(tok, h), sg_at(tok, h), dev(tok=far))
        t_sib[h].start(sg_at(tok, h), sg_at(tok, h), dev(tok=sib))

    def share_tokens(h):
        t_far[h].arrived()
        t_both[h].start(sg_at(far, h), sg_at(far, h), dev(tok=sib))

    basis_there(0, 0)
    add_range(0, y, True)
    basis_there(0, 1)
    for d in (1, 3):
        for j in range(4):
            if (j < 2) != (d == 1):
                g_y[j, d].arrived()
        add_range(0, dn(y, d))
    for j in range(4):
        g_f[j].arrived()
    add_range(0, up(y, 2))
    exchange_products(0)
    share_basis(1, 0)
    forward_sq(0)
    for j in three:
        s_x[j].arrived()
        spread_sq(j)
    basis_there(1, 0)
    add_range(1, y, True)
    add_range(1, dn(y, 1))
    square_products(0)
    forward_sq(1)
    share_basis(1, 1)
    basis_there(1, 1)
    add_range(1, up(y, 1))
    add_range(1, up(y, 2))
    exchange_products(1)
    share_tokens(0)
    forward_sq(3)
    square_products(1)
    forward_sq(2)
    for j in range(4):
        for d in (1, 3):
            if (j < 2) != (d == 1):
                s_y[j, d].arrived()
        s_f[j].arrived()

    tile = 256
    scale = 1.0 / (cols * NT)

    def add_tokens(t, first, final):
        for n in range(0, out.shape[1], tile):
            part = lax.dot_general(sg[t], sq[t, n:n + tile, :], (((1,), (1,)), ((), ())), preferred_element_type=F32)
            value = part if first else out[:, n:n + tile] + part
            out[:, n:n + tile] = value * scale if final else value

    add_tokens(tok, True, False)
    for h in range(2):
        t_sib[h].arrived()
    add_tokens(sib, False, False)
    share_tokens(1)
    add_tokens(far, False, False)
    for h in range(2):
        t_both[h].arrived()
    add_tokens(up(sib, 2), False, True)

    for cp in sent:
        cp.wait_send()


def body(acts_t, grads_t, basis_a, basis_g):
    da, cols = acts_t.shape
    dg = grads_t.shape[0]
    fa = basis_a.shape[1] // NY
    rows_a, quarter = NY * da, cols // NY
    fx, half = NZ * dg, dg // 2
    anywhere = pl.BlockSpec(memory_space=pl.ANY)
    n_out = basis_a.shape[1] // NT
    return pl.pallas_call(
        kernel,
        out_shape=jax.ShapeDtypeStruct((dg, n_out), F32),
        in_specs=[anywhere] * 4,
        out_specs=pl.BlockSpec(memory_space=pltpu.VMEM),
        scratch_shapes=[
            pltpu.VMEM((fa, cols), BF16),
            pltpu.VMEM((rows_a, fa), BF16),
            pltpu.VMEM((NY, rows_a, quarter), F32),
            pltpu.VMEM((NY - 1, rows_a, quarter), F32),
            pltpu.VMEM((rows_a, quarter), BF16),
            pltpu.VMEM((NT, n_out, cols), BF16),
            pltpu.VMEM((NY, fx, cols), BF16),
            pltpu.VMEM((2, NY, NX * half, fx), BF16),
            pltpu.VMEM((2, NX * half, cols), F32),
            pltpu.VMEM((2, NX * half, cols), BF16),
            pltpu.VMEM((2, NX - 1, half, cols), BF16),
            pltpu.VMEM((NT, dg, cols), BF16),
            pltpu.SemaphoreType.DMA((N_COPIES,)),
            pltpu.SemaphoreType.DMA((N_COPIES,)),
            pltpu.SemaphoreType.DMA((N_LOCAL,)),
        ],
        compiler_params=pltpu.CompilerParams(
            collective_id=0, has_side_effects=True, vmem_limit_bytes=60 * 2**20
        ),
    )(acts_t, grads_t, basis_a, basis_g)


def solution(mesh):
    return jax.shard_map(
        body,
        mesh=mesh,
        in_specs=(P("col", "tok"), P("col", "tok"), P("col", None), P("col", None)),
        out_specs=P("col", "tok"),
        check_vma=False,
    )
```

time: 1230 us -> 109 us (0.09)
  waiting for transfers between devices: 1200 us -> 0 us
  Pallas kernels: 0 us -> 105 us
  matrix products: 18.5 us -> 0 us
  between operations: 13.1 us -> 0.01 us
    all_gather x3 -> x0, waiting for transfers between devices: 1080 us -> none  [the longest x1 406 us: body(): lax.all_gather(grads_t, 'col', axis=0, tiled=True)]
    reduce_scatter x1 -> x0, waiting for transfers between devices: 111 us -> none  [body(): lax.psum_scatter(partial_tile, 'tok', scatter_dimension=1, tiled=True)]
    pallas_call x0 -> x1, Pallas kernels: none -> 105 us  [body(): pl.pallas_call(kernel, out_shape=jax.ShapeDtypeStruct((dg, n_out), F32),...]
    dot_general x2 -> x0, matrix products: 18.5 us -> none  [the longest x1 14.8 us: body(): lax.dot_general(sq_g, sq_full, (((1,), (1,)), ((), ())), preferred_elemen...]
  transfers between devices with their start and end apart: 4 -> 0, of which waited for: 4 -> 0; matrix products, arithmetic and copies ran while one was open for 0% -> 0% of each run, Pallas kernels for 0% -> 0%
where the time goes in v1:
time: 109 us; the launch traced here: 108 us
  Pallas kernels  105 us (96%)
  local copies, waits for them, and re-layouts  2.2 us (2%)
    pallas_call x1, Pallas kernels, body(): pl.pallas_call(kernel, out_shape=jax.ShapeDtypeStruct((dg, n_out), F32),...  105 us
    unnamed x1, local copies, waits for them, and re-layouts  2.2 us

profile of v1, /device:TPU:1, one launch (start us, length us, event | category | flops | bytes accessed | tf_op | source)
XLA Modules:
  0.0 107.5 jit_solution(2562873377113453813)
XLA Ops:
  0.0 105.3 %shard_map.46 = f32[224,1024]{1,0:T(8,128)} custom-call(bf16[64,512]{1,0:T(8,128)(2,1)} %acts.1, bf16[224,512]{1,0:T(8,128)(2,1)} %grads.1, bf16[64,4096]{1,0:T(8,128)(2,1)} %basis_a.1, bf16[224,14336]{1,0:T(8,128)(2,1)} %basis_g.1), custom_call_target="tpu_custom_call" | custom-call | tf_op jit(solution)/shard_map/pallas_call | solution.py:337
  105.3 2.2 %copy.6 = f32[224,1024]{1,0:T(8,128)} copy(f32[224,1024]{1,0:T(8,128)} %shard_map.46) | data formatting | bytes 1835008

commit v2 on v0

v2 whole, which is shorter than its diff:
```python
import jax
import jax.numpy as jnp
from jax import lax
from jax.experimental import pallas as pl
from jax.experimental.pallas import tpu as pltpu
from jax.sharding import PartitionSpec as P

MESH = pl.DeviceIdType.MESH
BF16 = jnp.bfloat16
F32 = jnp.float32
NX, NY, NZ, NT = 4, 4, 4, 4


class Sems:
    def __init__(self, send, recv):
        self.send, self.recv, self.used = send, recv, 0

    def take(self):
        i = self.used
        self.used += 1
        return self.send.at[i], self.recv.at[i]


N_COPIES = 128
N_LOCAL = 12

THREE = (1, 3, 2)
SIDES = (1, 3)


def way(j):
    return 1 if j < 2 else 3


SCHEDULE = (
    ("bx", 0, 0, 1), ("bx", 0, 0, 3), ("af", 0), ("gz", 2), ("as", 1), ("as", 3), ("as", 2), ("ax", 1), ("ax", 2),
    ("ax", 3), ("bs", 0, 0, 3), ("bs", 0, 0, 1), ("gf", 0), ("bx", 0, 1, 3), ("bx", 0, 1, 1), ("gz", 1), ("af", 2),
    ("af", 3), ("af", 1), ("gs", 2), ("bx", 0, 1, 2), ("pa",), ("bs", 0, 1, 1), ("gf", 2), ("gs", 1),
    ("bs", 0, 1, 3), ("gz", 3), ("bx", 0, 0, 2), ("bs", 0, 1, 2), ("bx", 1, 0, 1), ("bx", 1, 0, 3), ("bs", 0, 0, 2),
    ("bx", 1, 1, 2), ("sa",), ("bs", 1, 0, 3), ("bs", 1, 0, 1), ("gs", 3), ("cg", 0, 0), ("gf", 1), ("bx", 1, 1, 1),
    ("bx", 1, 1, 3), ("bs", 1, 1, 2), ("bx", 1, 0, 2), ("sx",), ("bs", 1, 1, 1), ("bs", 1, 1, 3), ("gf", 3),
    ("uf", 0), ("cg", 0, 1), ("cg", 0, 2), ("us", 2), ("sf", 0), ("ss", 3), ("sxf", 1), ("bs", 1, 0, 2), ("uf", 2),
    ("sxf", 0), ("ss", 1), ("cg", 0, 3), ("cg", 1, 0), ("cg", 1, 1), ("ss", 2), ("cg", 1, 2), ("cg", 1, 3),
    ("sf", 3), ("sq", 0), ("sq", 1), ("us", 1), ("us", 3), ("sf", 1), ("sf", 2), ("tb", 0), ("uf", 1), ("uf", 3),
    ("tb", 1), ("fin", 0), ("fin", 1), ("fin", 2), ("fin", 3),
)


SPLIT = 3


def kernel(acts, grads, basis_a, basis_g, out, xa, ba, pa, ra, sa, sq, xg, bg, acc, ps, pr, sg,
           send_sem, recv_sem, local_sem):
    tok = lax.axis_index("tok")
    col = lax.axis_index("col")
    zl = lax.rem(col, 4)
    x = lax.rem(lax.div(col, 4), 4)
    y = lax.div(col, 16)
    c = lax.rem(tok, 2)
    da, fa = acts.shape[0], basis_a.shape[1] // NY
    dg = grads.shape[0]
    half = dg // 2
    fx = NZ * dg
    fy = NX * fx
    cols = acts.shape[1]
    quarter = cols // NY

    def up(v, d):
        return lax.rem(v + d, 4)

    def dn(v, d):
        return lax.rem(v + 4 - d, 4)

    def dev(tok=tok, y=y, x=x, zl=zl):
        return (tok, (y * 4 + x) * 4 + zl)

    sib = tok + 1 - 2 * c
    far = up(tok, 2)

    barrier = pltpu.get_barrier_semaphore()
    partners = [dev(tok=up(tok, dt), zl=up(zl, dz)) for dt in range(4) for dz in range(4) if dt or dz]
    partners += [dev(x=up(x, d)) for d in (1, 2, 3)] + [dev(y=up(y, d)) for d in (1, 2, 3)]
    for p in partners:
        pl.semaphore_signal(barrier, inc=1, device_id=p, device_id_type=MESH)
    pl.semaphore_wait(barrier, len(partners))

    sems = Sems(send_sem, recv_sem)
    sent = []

    class Copy:
        def __init__(self, tag, landing):
            self.tag, self.landing, self.sems, self.here = tag, landing, sems.take(), False

        def start(self, src, dst, to):
            s, r = self.sems
            cp = pltpu.make_async_remote_copy(src_ref=src, dst_ref=dst, send_sem=s, recv_sem=r,
                                              device_id=to, device_id_type=MESH)
            cp.start()
            sent.append(cp)

        def arrived(self):
            if self.here:
                return
            self.here = True
            s, r = self.sems
            pltpu.make_async_remote_copy(src_ref=self.landing, dst_ref=self.landing, send_sem=s, recv_sem=r,
                                         device_id=dev(), device_id_type=MESH).wait_recv()

    n_local = [0]

    def local(src, dst):
        cp = pltpu.make_async_copy(src, dst, local_sem.at[n_local[0]])
        n_local[0] += 1
        cp.start()
        return cp

    def xa_at(xs, zs):
        return xa.at[pl.ds(pl.multiple_of(xs * (NZ * da) + zs * da, da), da), :]

    def ba_at(ys, core):
        return ba.at[pl.ds(pl.multiple_of(ys * da + core * (da // 2), da // 2), da // 2), :]

    def ba_cols(ys):
        return pl.ds(pl.multiple_of(ys * fa, fa), fa)

    def xg_at(ys, zs):
        return xg.at[ys, pl.ds(pl.multiple_of(zs * dg, 32), dg), :]

    def bg_at(h, ys, xs):
        return bg.at[h, ys, pl.ds(pl.multiple_of(xs * half, 16), half), :]

    def bg_cols(h, ys, xs):
        return basis_g.at[h * half:(h + 1) * half, pl.ds(pl.multiple_of(ys * fy + xs * fx, 128), fx)]

    def lanes(q):
        return pl.ds(pl.multiple_of(q * quarter, quarter), quarter)

    def sq_block(t, xs, zs, q):
        return sq.at[t, pl.ds(pl.multiple_of((xs * NZ + zs) * da, da), da), lanes(q)]

    def sq_chunk(xs, q, first=0, rows=NZ * da):
        return sq.at[0:SPLIT, pl.ds(pl.multiple_of(xs * (NZ * da) + first, 128), rows), lanes(q)]

    def sq_rest(xs, q):
        return sq.at[SPLIT:NT, pl.ds(pl.multiple_of(xs * (NZ * da), NZ * da), NZ * da), lanes(q)]

    a_z = {d: Copy("a_z", xa_at(x, dn(zl, d))) for d in THREE}
    a_x = {(j, d): Copy("a_x", xa_at(dn(x, d), dn(zl, j))) for j in range(4) for d in SIDES}
    a_f = {j: Copy("a_f", xa_at(up(x, 2), dn(zl, j))) for j in range(4)}
    b_a = {d: Copy("b_a", ba_at(dn(y, d), c)) for d in THREE}
    a_s = {d: Copy("a_s", ba_at(dn(y, d), 1 - c)) for d in THREE}
    p_a = {d: Copy("p_a", ra.at[d - 1]) for d in THREE}
    g_z = {d: Copy("g_z", xg_at(y, dn(zl, d))) for d in THREE}
    g_y = {(j, d): Copy("g_y", xg_at(dn(y, d), dn(zl, j))) for j in range(4) for d in SIDES}
    g_f = {j: Copy("g_f", xg_at(up(y, 2), dn(zl, j))) for j in range(4)}
    mine = [up(y, 3 * c), up(y, 1 + c)]
    theirs = [up(y, 3 * (1 - c)), up(y, 2 - c)]
    pieces = [(h, k, d) for h in range(2) for k in range(2) for d in THREE]
    b_x = {(h, k, d): Copy("b_x", bg_at(h, mine[k], dn(x, d))) for h, k, d in pieces}
    b_s = {(h, k, d): Copy("b_s", bg_at(h, theirs[k], dn(x, d))) for h, k, d in pieces}
    p_g = {(h, d): Copy("p_g", pr.at[h, d - 1]) for h in range(2) for d in THREE}
    turns = [(dt, dz) for dt in range(4) for dz in range(4) if dt or dz]
    s_z = {(dt, dz): Copy("s_z", sq_block(dn(tok, dt), x, dn(zl, dz), y)) for dt, dz in turns}
    s_x = {d: Copy("s_x", sq_chunk(dn(x, d), y)) for d in SIDES}
    s_xf = [Copy("s_xf", sq_chunk(up(x, 2), y, 128 * i, 128)) for i in range(2)]
    s_y = {(j, d): Copy("s_y", sq_chunk(dn(x, j), dn(y, d))) for j in range(4) for d in SIDES}
    s_f = {j: Copy("s_f", sq_chunk(dn(x, j), up(y, 2))) for j in range(4)}
    u_y = {d: Copy("u_y", sq_rest(x, dn(y, d))) for d in THREE}
    u_x = {(j, d): Copy("u_x", sq_rest(dn(x, d), dn(y, j))) for j in range(4) for d in SIDES}
    u_f = {j: Copy("u_f", sq_rest(up(x, 2), dn(y, j))) for j in range(4)}

    def sg_at(t, h):
        return sg.at[t, h * half:(h + 1) * half, :]

    t_far = [Copy("t_far", sg_at(far, h)) for h in range(2)]
    t_sib = [Copy("t_sib", sg_at(sib, h)) for h in range(2)]
    t_both = [Copy("t_both", sg_at(up(sib, 2), h)) for h in range(2)]

    def all_of(*groups):
        for group in groups:
            for copy in group.values() if isinstance(group, dict) else group:
                copy.arrived()

    for d in THREE:
        a_z[d].start(acts, xa_at(x, zl), dev(zl=up(zl, d)))
    for d in SIDES:
        a_x[0, d].start(acts, xa_at(x, zl), dev(x=up(x, d)))
    for d in THREE:
        b_a[d].start(basis_a.at[pl.ds(pl.multiple_of(c * (da // 2), da // 2), da // 2), ba_cols(up(y, d))], ba_at(y, c),
                     dev(y=up(y, d)))
    for d in SIDES:
        g_y[0, d].start(grads, xg_at(y, zl), dev(y=up(y, d)))
    own_a = [local(acts, xa_at(x, zl)), local(basis_a.at[:, ba_cols(y)], ba.at[pl.ds(pl.multiple_of(y * da, da), da), :])]
    own_g = [local(grads, xg_at(y, zl))]
    own_g += [local(bg_cols(h, ys, x), bg_at(h, ys, x)) for h in range(2) for ys in mine + theirs]
    own_s = []

    def ax(j):
        a_z[j].arrived()
        for d in SIDES:
            a_x[j, d].start(xa_at(x, dn(zl, j)), xa_at(x, dn(zl, j)), dev(x=up(x, d)))

    def af(j):
        d = way(j)
        a_x[j, d].arrived()
        a_f[j].start(xa_at(dn(x, d), dn(zl, j)), xa_at(dn(x, d), dn(zl, j)), dev(x=up(x, d)))

    def share_a(d):
        b_a[d].arrived()
        a_s[d].start(ba_at(dn(y, d), c), ba_at(dn(y, d), c), dev(tok=sib))

    def project_a():
        for cp in own_a:
            cp.wait()
        all_of(a_x, a_f, b_a, a_s)
        for ys in range(NY):
            pa[ys] = jnp.dot(ba[...], xa[:, ys * quarter:(ys + 1) * quarter], preferred_element_type=F32)
        for d in THREE:
            p_a[d].start(pa.at[up(y, d)], ra.at[d - 1], dev(y=up(y, d)))

    def square_a():
        all_of(p_a)
        total = pa[y] + ra[0] + ra[1] + ra[2]
        sa[...] = (total * total).astype(BF16)
        for dt, dz in turns:
            t = up(tok, dt)
            s_z[dt, dz].start(sa.at[pl.ds(pl.multiple_of(t * da, da), da), :], sq_block(tok, x, zl, y),
                              dev(tok=t, zl=up(zl, dz)))
        own_s.append(local(sa.at[pl.ds(pl.multiple_of(tok * da, da), da), :], sq_block(tok, x, zl, y)))

    def spread(j):
        for d in SIDES:
            s_y[j, d].start(sq_chunk(dn(x, j), y), sq_chunk(dn(x, j), y), dev(y=up(y, d)))

    def spread_rest(j):
        for d in SIDES:
            u_x[j, d].start(sq_rest(x, dn(y, j)), sq_rest(x, dn(y, j)), dev(x=up(x, d)))

    def sx():
        own_s[0].wait()
        all_of(s_z)
        for d in SIDES:
            s_x[d].start(sq_chunk(x, y), sq_chunk(x, y), dev(x=up(x, d)))
        spread(0)
        for d in THREE:
            u_y[d].start(sq_rest(x, y), sq_rest(x, y), dev(y=up(y, d)))
        spread_rest(0)

    def sxf(i):
        d = SIDES[i]
        s_x[d].arrived()
        part = sq_chunk(dn(x, d), y, 128 * i, 128)
        s_xf[i].start(part, part, dev(x=up(x, d)))

    def ss(j):
        all_of(s_xf if j == 2 else [s_x[j]])
        spread(j)

    def sf(j):
        d = way(j)
        s_y[j, d].arrived()
        s_f[j].start(sq_chunk(dn(x, j), dn(y, d)), sq_chunk(dn(x, j), dn(y, d)), dev(y=up(y, d)))

    def us(j):
        u_y[j].arrived()
        spread_rest(j)

    def uf(j):
        d = way(j)
        u_x[j, d].arrived()
        u_f[j].start(sq_rest(dn(x, d), dn(y, j)), sq_rest(dn(x, d), dn(y, j)), dev(x=up(x, d)))

    def gz(d):
        g_z[d].start(grads, xg_at(y, zl), dev(zl=up(zl, d)))

    def gs(j):
        g_z[j].arrived()
        for d in SIDES:
            g_y[j, d].start(xg_at(y, dn(zl, j)), xg_at(y, dn(zl, j)), dev(y=up(y, d)))

    def gf(j):
        d = way(j)
        g_y[j, d].arrived()
        g_f[j].start(xg_at(dn(y, d), dn(zl, j)), xg_at(dn(y, d), dn(zl, j)), dev(y=up(y, d)))

    def bx(h, k, d):
        b_x[h, k, d].start(bg_cols(h, mine[k], up(x, d)), bg_at(h, mine[k], x), dev(x=up(x, d)))

    def bs(h, k, d):
        b_x[h, k, d].arrived()
        b_s[h, k, d].start(bg_at(h, mine[k], dn(x, d)), bg_at(h, mine[k], dn(x, d)), dev(tok=sib))

    def cg(h, i):
        while own_g:
            own_g.pop().wait()
        for d in THREE:
            all_of([b_x[h, i // 2, d], b_s[h, i // 2, d]])
        if i == 0:
            all_of(g_z)
        elif i == 3:
            all_of(g_f)
        else:
            all_of([g_y[j, SIDES[i - 1]] for j in range(4)])
        ys = (y, dn(y, 1), up(y, 1), up(y, 2))[i]
        part = jnp.dot(bg[h, ys], xg[ys], preferred_element_type=F32)
        acc[h] = part if i == 0 else acc[h] + part
        if i == 3:
            ps[h] = acc[h].astype(BF16)
            for d in (2, 1, 3):
                xs = up(x, d)
                p_g[h, d].start(ps.at[h, pl.ds(pl.multiple_of(xs * half, 16), half), :], pr.at[h, d - 1], dev(x=xs))

    def square_g(h):
        all_of([p_g[h, d] for d in THREE])
        own = acc[h, pl.ds(pl.multiple_of(x * half, 8), half), :]
        total = own + pr[h, 0].astype(F32) + pr[h, 1].astype(F32) + pr[h, 2].astype(F32)
        sg[tok, h * half:(h + 1) * half, :] = (total * total).astype(BF16)
        t_far[h].start(sg_at(tok, h), sg_at(tok, h), dev(tok=far))
        t_sib[h].start(sg_at(tok, h), sg_at(tok, h), dev(tok=sib))

    def tb(h):
        t_far[h].arrived()
        t_both[h].start(sg_at(far, h), sg_at(far, h), dev(tok=sib))

    tile = 256
    scale = 1.0 / (cols * NT)

    def fin(i):
        all_of(*((s_x, s_xf, s_y, s_f, u_y, u_x, u_f), (t_sib,), (t_far,), (t_both,))[i])
        t = (tok, sib, far, up(sib, 2))[i]
        for n in range(0, out.shape[1], tile):
            part = lax.dot_general(sg[t], sq[t, n:n + tile, :], (((1,), (1,)), ((), ())), preferred_element_type=F32)
            value = part if i == 0 else out[:, n:n + tile] + part
            out[:, n:n + tile] = value * scale if i == 3 else value

    steps = {"ax": ax, "af": af, "as": share_a, "pa": project_a, "sa": square_a, "sx": sx, "sxf": sxf, "ss": ss, "sf": sf,
             "us": us, "uf": uf, "gz": gz, "gs": gs, "gf": gf, "bx": bx, "bs": bs, "cg": cg, "sq": square_g, "tb": tb,
             "fin": fin}
    for name, *where in SCHEDULE:
        steps[name](*where)

    for cp in sent:
        cp.wait_send()


def body(acts_t, grads_t, basis_a, basis_g):
    da, cols = acts_t.shape
    dg = grads_t.shape[0]
    fa = basis_a.shape[1] // NY
    rows_a, quarter = NY * da, cols // NY
    fx, half = NZ * dg, dg // 2
    anywhere = pl.BlockSpec(memory_space=pl.ANY)
    n_out = basis_a.shape[1] // NT
    return pl.pallas_call(
        kernel,
        out_shape=jax.ShapeDtypeStruct((dg, n_out), F32),
        in_specs=[anywhere] * 4,
        out_specs=pl.BlockSpec(memory_space=pltpu.VMEM),
        scratch_shapes=[
            pltpu.VMEM((fa, cols), BF16),
            pltpu.VMEM((rows_a, fa), BF16),
            pltpu.VMEM((NY, rows_a, quarter), F32),
            pltpu.VMEM((NY - 1, rows_a, quarter), F32),
            pltpu.VMEM((rows_a, quarter), BF16),
            pltpu.VMEM((NT, n_out, cols), BF16),
            pltpu.VMEM((NY, fx, cols), BF16),
            pltpu.VMEM((2, NY, NX * half, fx), BF16),
            pltpu.VMEM((2, NX * half, cols), F32),
            pltpu.VMEM((2, NX * half, cols), BF16),
            pltpu.VMEM((2, NX - 1, half, cols), BF16),
            pltpu.VMEM((NT, dg, cols), BF16),
            pltpu.SemaphoreType.DMA((N_COPIES,)),
            pltpu.SemaphoreType.DMA((N_COPIES,)),
            pltpu.SemaphoreType.DMA((N_LOCAL,)),
        ],
        compiler_params=pltpu.CompilerParams(
            collective_id=0, has_side_effects=True, vmem_limit_bytes=60 * 2**20
        ),
    )(acts_t, grads_t, basis_a, basis_g)


def solution(mesh):
    return jax.shard_map(
        body,
        mesh=mesh,
        in_specs=(P("col", "tok"), P("col", "tok"), P("col", None), P("col", None)),
        out_specs=P("col", "tok"),
        check_vma=False,
    )
```

time: 1230 us -> 104 us (0.08)
  waiting for transfers between devices: 1200 us -> 0 us
  Pallas kernels: 0 us -> 101 us
  matrix products: 18.5 us -> 0 us
  between operations: 13.1 us -> 0.01 us
    all_gather x3 -> x0, waiting for transfers between devices: 1080 us -> none  [the longest x1 406 us: body(): lax.all_gather(grads_t, 'col', axis=0, tiled=True)]
    reduce_scatter x1 -> x0, waiting for transfers between devices: 111 us -> none  [body(): lax.psum_scatter(partial_tile, 'tok', scatter_dimension=1, tiled=True)]
    pallas_call x0 -> x1, Pallas kernels: none -> 101 us  [body(): pl.pallas_call(kernel, out_shape=jax.ShapeDtypeStruct((dg, n_out), F32),...]
    dot_general x2 -> x0, matrix products: 18.5 us -> none  [the longest x1 14.8 us: body(): lax.dot_general(sq_g, sq_full, (((1,), (1,)), ((), ())), preferred_elemen...]
  transfers between devices with their start and end apart: 4 -> 0, of which waited for: 4 -> 0; matrix products, arithmetic and copies ran while one was open for 0% -> 0% of each run, Pallas kernels for 0% -> 0%
where the time goes in v2:
time: 104 us
  Pallas kernels  101 us (97%)
  local copies, waits for them, and re-layouts  2.2 us (2%)
    pallas_call x1, Pallas kernels, body(): pl.pallas_call(kernel, out_shape=jax.ShapeDtypeStruct((dg, n_out), F32),...  101 us
    unnamed x1, local copies, waits for them, and re-layouts  2.2 us

profile of v2, /device:TPU:1, one launch (start us, length us, event | category | flops | bytes accessed | tf_op | source)
XLA Modules:
  0.0 103.6 jit_solution(12351317332212008753)
XLA Ops:
  0.0 101.4 %shard_map.46 = f32[224,1024]{1,0:T(8,128)} custom-call(bf16[64,512]{1,0:T(8,128)(2,1)} %acts.1, bf16[224,512]{1,0:T(8,128)(2,1)} %grads.1, bf16[64,4096]{1,0:T(8,128)(2,1)} %basis_a.1, bf16[224,14336]{1,0:T(8,128)(2,1)} %basis_g.1), custom_call_target="tpu_custom_call" | custom-call | tf_op jit(solution)/shard_map/pallas_call | solution.py:354
  101.4 2.2 %copy.6 = f32[224,1024]{1,0:T(8,128)} copy(f32[224,1024]{1,0:T(8,128)} %shard_map.46) | data formatting | bytes 1835008

commit v3 on v2

--- a/solution.py
+++ b/solution.py
@@ -21,8 +21,8 @@
         return self.send.at[i], self.recv.at[i]
 
 
-N_COPIES = 128
-N_LOCAL = 12
+N_COPIES = 144
+N_LOCAL = 24
 
 THREE = (1, 3, 2)
 SIDES = (1, 3)
@@ -33,20 +33,23 @@
 
 
 SCHEDULE = (
-    ("bx", 0, 0, 1), ("bx", 0, 0, 3), ("af", 0), ("gz", 2), ("as", 1), ("as", 3), ("as", 2), ("ax", 1), ("ax", 2),
-    ("ax", 3), ("bs", 0, 0, 3), ("bs", 0, 0, 1), ("gf", 0), ("bx", 0, 1, 3), ("bx", 0, 1, 1), ("gz", 1), ("af", 2),
-    ("af", 3), ("af", 1), ("gs", 2), ("bx", 0, 1, 2), ("pa",), ("bs", 0, 1, 1), ("gf", 2), ("gs", 1),
-    ("bs", 0, 1, 3), ("gz", 3), ("bx", 0, 0, 2), ("bs", 0, 1, 2), ("bx", 1, 0, 1), ("bx", 1, 0, 3), ("bs", 0, 0, 2),
-    ("bx", 1, 1, 2), ("sa",), ("bs", 1, 0, 3), ("bs", 1, 0, 1), ("gs", 3), ("cg", 0, 0), ("gf", 1), ("bx", 1, 1, 1),
-    ("bx", 1, 1, 3), ("bs", 1, 1, 2), ("bx", 1, 0, 2), ("sx",), ("bs", 1, 1, 1), ("bs", 1, 1, 3), ("gf", 3),
-    ("uf", 0), ("cg", 0, 1), ("cg", 0, 2), ("us", 2), ("sf", 0), ("ss", 3), ("sxf", 1), ("bs", 1, 0, 2), ("uf", 2),
-    ("sxf", 0), ("ss", 1), ("cg", 0, 3), ("cg", 1, 0), ("cg", 1, 1), ("ss", 2), ("cg", 1, 2), ("cg", 1, 3),
-    ("sf", 3), ("sq", 0), ("sq", 1), ("us", 1), ("us", 3), ("sf", 1), ("sf", 2), ("tb", 0), ("uf", 1), ("uf", 3),
-    ("tb", 1), ("fin", 0), ("fin", 1), ("fin", 2), ("fin", 3),
+    ("bx", 0, 0, 2), ("ax", 1), ("gz", 2), ("ax", 3), ("gf", 0), ("ax", 2), ("af", 0), ("af", 3), ("af", 1),
+    ("as", 3), ("af", 2), ("vz", 0), ("gs", 2), ("as", 2), ("bx", 0, 0, 1), ("gz", 1), ("bx", 0, 0, 3),
+    ("bx", 1, 0, 1), ("bs", 0, 0, 2), ("as", 1), ("pa",), ("bx", 1, 0, 3), ("gf", 2), ("gz", 3), ("bx", 0, 1, 1),
+    ("bx", 0, 1, 3), ("gs", 1), ("bs", 0, 0, 1), ("bx", 1, 1, 2), ("sa",), ("gs", 3), ("bx", 0, 1, 2),
+    ("bs", 0, 0, 3), ("bs", 0, 1, 3), ("sx",), ("bs", 0, 1, 1), ("vz", 3), ("vz", 1), ("bs", 0, 1, 2), ("gf", 3),
+    ("gf", 1), ("bx", 1, 0, 2), ("cg", 0, 0), ("vz", 2), ("sxf", 1), ("sxf", 0), ("bs", 1, 1, 2), ("bx", 1, 1, 3),
+    ("bs", 1, 0, 3), ("bs", 1, 0, 1), ("cg", 0, 1), ("ss", 3), ("bx", 1, 1, 1), ("cg", 0, 2), ("cg", 0, 3),
+    ("bs", 1, 0, 2), ("ss", 2), ("bs", 1, 1, 1), ("ss", 1), ("cg", 1, 0), ("sf", 3), ("cg", 1, 1), ("bs", 1, 1, 3),
+    ("cg", 1, 2), ("us", 2), ("sf", 0), ("us", 1), ("cg", 1, 3), ("us", 3), ("sq", 0), ("sf", 2), ("sf", 1),
+    ("uf", 1), ("uf", 2), ("sq", 1), ("uf", 3), ("uf", 0), ("tb", 0), ("fin", 0), ("tb", 1), ("fin", 1), ("fin", 2),
+    ("fin", 3),
 )
 
 
 SPLIT = 3
+PARTS = (160, 64)
+FLIP = 32
 
 
 def kernel(acts, grads, basis_a, basis_g, out, xa, ba, pa, ra, sa, sq, xg, bg, acc, ps, pr, sg,
@@ -59,7 +62,8 @@
     c = lax.rem(tok, 2)
     da, fa = acts.shape[0], basis_a.shape[1] // NY
     dg = grads.shape[0]
-    half = dg // 2
+    at = [sum(PARTS[:h]) for h in range(len(PARTS))]
+    flip = FLIP
     fx = NZ * dg
     fy = NX * fx
     cols = acts.shape[1]
@@ -124,13 +128,25 @@
         return pl.ds(pl.multiple_of(ys * fa, fa), fa)
 
     def xg_at(ys, zs):
-        return xg.at[ys, pl.ds(pl.multiple_of(zs * dg, 32), dg), :]
+        return xg.at[ys, pl.ds(pl.multiple_of(zs * dg, 32), dg - flip), :]
+
+    def xv_at(ys, zs):
+        return xg.at[ys, pl.ds(pl.multiple_of(zs * dg + (dg - flip), 32), flip), :]
 
     def bg_at(h, ys, xs):
-        return bg.at[h, ys, pl.ds(pl.multiple_of(xs * half, 16), half), :]
+        return bg.at[ys, pl.ds(pl.multiple_of(NX * at[h] + xs * PARTS[h], 16), PARTS[h]), :]
 
     def bg_cols(h, ys, xs):
-        return basis_g.at[h * half:(h + 1) * half, pl.ds(pl.multiple_of(ys * fy + xs * fx, 128), fx)]
+        return basis_g.at[at[h]:at[h] + PARTS[h], pl.ds(pl.multiple_of(ys * fy + xs * fx, 128), fx)]
+
+    def part_rows(h, xs):
+        return pl.ds(pl.multiple_of(NX * at[h] + xs * PARTS[h], 16), PARTS[h])
+
+    def rows_of(h):
+        return pl.ds(at[h], PARTS[h])
+
+    parts = range(len(PARTS))
+    main, rest = grads.at[0:dg - flip, :], grads.at[dg - flip:dg, :]
 
     def lanes(q):
         return pl.ds(pl.multiple_of(q * quarter, quarter), quarter)
@@ -153,12 +169,14 @@
     g_z = {d: Copy("g_z", xg_at(y, dn(zl, d))) for d in THREE}
     g_y = {(j, d): Copy("g_y", xg_at(dn(y, d), dn(zl, j))) for j in range(4) for d in SIDES}
     g_f = {j: Copy("g_f", xg_at(up(y, 2), dn(zl, j))) for j in range(4)}
+    v_y = {d: Copy("v_y", xv_at(dn(y, d), zl)) for d in THREE}
+    v_z = {(i, d): Copy("v_z", xv_at(dn(y, i), dn(zl, d))) for i in range(4) for d in THREE}
     mine = [up(y, 3 * c), up(y, 1 + c)]
     theirs = [up(y, 3 * (1 - c)), up(y, 2 - c)]
-    pieces = [(h, k, d) for h in range(2) for k in range(2) for d in THREE]
+    pieces = [(h, k, d) for h in parts for k in range(2) for d in THREE]
     b_x = {(h, k, d): Copy("b_x", bg_at(h, mine[k], dn(x, d))) for h, k, d in pieces}
     b_s = {(h, k, d): Copy("b_s", bg_at(h, theirs[k], dn(x, d))) for h, k, d in pieces}
-    p_g = {(h, d): Copy("p_g", pr.at[h, d - 1]) for h in range(2) for d in THREE}
+    p_g = {(h, d): Copy("p_g", pr.at[d - 1, rows_of(h), :]) for h in parts for d in THREE}
     turns = [(dt, dz) for dt in range(4) for dz in range(4) if dt or dz]
     s_z = {(dt, dz): Copy("s_z", sq_block(dn(tok, dt), x, dn(zl, dz), y)) for dt, dz in turns}
     s_x = {d: Copy("s_x", sq_chunk(dn(x, d), y)) for d in SIDES}
@@ -170,11 +188,11 @@
     u_f = {j: Copy("u_f", sq_rest(up(x, 2), dn(y, j))) for j in range(4)}
 
     def sg_at(t, h):
-        return sg.at[t, h * half:(h + 1) * half, :]
-
-    t_far = [Copy("t_far", sg_at(far, h)) for h in range(2)]
-    t_sib = [Copy("t_sib", sg_at(sib, h)) for h in range(2)]
-    t_both = [Copy("t_both", sg_at(up(sib, 2), h)) for h in range(2)]
+        return sg.at[t, rows_of(h), :]
+
+    t_far = [Copy("t_far", sg_at(far, h)) for h in parts]
+    t_sib = [Copy("t_sib", sg_at(sib, h)) for h in parts]
+    t_both = [Copy("t_both", sg_at(up(sib, 2), h)) for h in parts]
 
     def all_of(*groups):
         for group in groups:
@@ -189,10 +207,12 @@
         b_a[d].start(basis_a.at[pl.ds(pl.multiple_of(c * (da // 2), da // 2), da // 2), ba_cols(up(y, d))], ba_at(y, c),
                      dev(y=up(y, d)))
     for d in SIDES:
-        g_y[0, d].start(grads, xg_at(y, zl), dev(y=up(y, d)))
+        g_y[0, d].start(main, xg_at(y, zl), dev(y=up(y, d)))
+    for d in THREE:
+        v_y[d].start(rest, xv_at(y, zl), dev(y=up(y, d)))
     own_a = [local(acts, xa_at(x, zl)), local(basis_a.at[:, ba_cols(y)], ba.at[pl.ds(pl.multiple_of(y * da, da), da), :])]
-    own_g = [local(grads, xg_at(y, zl))]
-    own_g += [local(bg_cols(h, ys, x), bg_at(h, ys, x)) for h in range(2) for ys in mine + theirs]
+    own_g = [local(grads, xg.at[y, pl.ds(pl.multiple_of(zl * dg, 32), dg), :])]
+    own_g += [local(bg_cols(h, ys, x), bg_at(h, ys, x)) for h in parts for ys in mine + theirs]
     own_s = []
 
     def ax(j):
@@ -271,7 +291,7 @@
         u_f[j].start(sq_rest(dn(x, d), dn(y, j)), sq_rest(dn(x, d), dn(y, j)), dev(x=up(x, d)))
 
     def gz(d):
-        g_z[d].start(grads, xg_at(y, zl), dev(zl=up(zl, d)))
+        g_z[d].start(main, xg_at(y, zl), dev(zl=up(zl, d)))
 
     def gs(j):
         g_z[j].arrived()
@@ -282,6 +302,12 @@
         d = way(j)
         g_y[j, d].arrived()
         g_f[j].start(xg_at(dn(y, d), dn(zl, j)), xg_at(dn(y, d), dn(zl, j)), dev(y=up(y, d)))
+
+    def vz(i):
+        if i:
+            v_y[i].arrived()
+        for d in THREE:
+            v_z[i, d].start(xv_at(dn(y, i), zl) if i else rest, xv_at(dn(y, i), zl), dev(zl=up(zl, d)))
 
     def bx(h, k, d):
         b_x[h, k, d].start(bg_cols(h, mine[k], up(x, d)), bg_at(h, mine[k], x), dev(x=up(x, d)))
@@ -295,26 +321,30 @@
             own_g.pop().wait()
         for d in THREE:
             all_of([b_x[h, i // 2, d], b_s[h, i // 2, d]])
+        ring = (0, 1, 3, 2)[i]
         if i == 0:
             all_of(g_z)
         elif i == 3:
             all_of(g_f)
         else:
-            all_of([g_y[j, SIDES[i - 1]] for j in range(4)])
-        ys = (y, dn(y, 1), up(y, 1), up(y, 2))[i]
-        part = jnp.dot(bg[h, ys], xg[ys], preferred_element_type=F32)
-        acc[h] = part if i == 0 else acc[h] + part
+            all_of([g_y[j, ring] for j in range(4)])
+        all_of([v_z[ring, d] for d in THREE], [v_y[ring]] if ring else [])
+        ys = dn(y, ring)
+        rows = slice(NX * at[h], NX * (at[h] + PARTS[h]))
+        part = jnp.dot(bg[ys, rows, :], xg[ys], preferred_element_type=F32)
+        acc[rows, :] = part if i == 0 else acc[rows, :] + part
         if i == 3:
-            ps[h] = acc[h].astype(BF16)
+            ps[rows, :] = acc[rows, :].astype(BF16)
             for d in (2, 1, 3):
                 xs = up(x, d)
-                p_g[h, d].start(ps.at[h, pl.ds(pl.multiple_of(xs * half, 16), half), :], pr.at[h, d - 1], dev(x=xs))
+                p_g[h, d].start(ps.at[part_rows(h, xs), :], pr.at[d - 1, rows_of(h), :], dev(x=xs))
 
     def square_g(h):
         all_of([p_g[h, d] for d in THREE])
-        own = acc[h, pl.ds(pl.multiple_of(x * half, 8), half), :]
-        total = own + pr[h, 0].astype(F32) + pr[h, 1].astype(F32) + pr[h, 2].astype(F32)
-        sg[tok, h * half:(h + 1) * half, :] = (total * total).astype(BF16)
+        total = acc[part_rows(h, x), :]
+        for d in range(NX - 1):
+            total = total + pr[d, rows_of(h), :].astype(F32)
+        sg[tok, rows_of(h), :] = (total * total).astype(BF16)
         t_far[h].start(sg_at(tok, h), sg_at(tok, h), dev(tok=far))
         t_sib[h].start(sg_at(tok, h), sg_at(tok, h), dev(tok=sib))
 
@@ -334,7 +364,7 @@
             out[:, n:n + tile] = value * scale if i == 3 else value
 
     steps = {"ax": ax, "af": af, "as": share_a, "pa": project_a, "sa": square_a, "sx": sx, "sxf": sxf, "ss": ss, "sf": sf,
-             "us": us, "uf": uf, "gz": gz, "gs": gs, "gf": gf, "bx": bx, "bs": bs, "cg": cg, "sq": square_g, "tb": tb,
+             "us": us, "uf": uf, "gz": gz, "gs": gs, "gf": gf, "vz": vz, "bx": bx, "bs": bs, "cg": cg, "sq": square_g, "tb": tb,
              "fin": fin}
     for name, *where in SCHEDULE:
         steps[name](*where)
@@ -348,7 +378,7 @@
     dg = grads_t.shape[0]
     fa = basis_a.shape[1] // NY
     rows_a, quarter = NY * da, cols // NY
-    fx, half = NZ * dg, dg // 2
+    fx = NZ * dg
     anywhere = pl.BlockSpec(memory_space=pl.ANY)
     n_out = basis_a.shape[1] // NT
     return pl.pallas_call(
@@ -364,10 +394,10 @@
             pltpu.VMEM((rows_a, quarter), BF16),
             pltpu.VMEM((NT, n_out, cols), BF16),
             pltpu.VMEM((NY, fx, cols), BF16),
-            pltpu.VMEM((2, NY, NX * half, fx), BF16),
-            pltpu.VMEM((2, NX * half, cols), F32),
-            pltpu.VMEM((2, NX * half, cols), BF16),
-            pltpu.VMEM((2, NX - 1, half, cols), BF16),
+            pltpu.VMEM((NY, NX * dg, fx), BF16),
+            pltpu.VMEM((NX * dg, cols), F32),
+            pltpu.VMEM((NX * dg, cols), BF16),
+            pltpu.VMEM((NX - 1, dg, cols), BF16),
             pltpu.VMEM((NT, dg, cols), BF16),
             pltpu.SemaphoreType.DMA((N_COPIES,)),
             pltpu.SemaphoreType.DMA((N_COPIES,)),

time: 104 us -> 92.2 us (0.89)
  Pallas kernels: 101 us -> 89.2 us
    pallas_call x1, Pallas kernels: 101 us -> 89.2 us  [body(): pl.pallas_call(kernel, out_shape=jax.ShapeDtypeStruct((dg, n_out), F32),...]
where the time goes in v3:
time: 92.2 us; the launch traced here: 91.5 us
  Pallas kernels  89.2 us (97%)
  local copies, waits for them, and re-layouts  2.2 us (2%)
    pallas_call x1, Pallas kernels, body(): pl.pallas_call(kernel, out_shape=jax.ShapeDtypeStruct((dg, n_out), F32),...  89.2 us
    unnamed x1, local copies, waits for them, and re-layouts  2.2 us

profile of v3, /device:TPU:1, one launch (start us, length us, event | category | flops | bytes accessed | tf_op | source)
XLA Modules:
  0.0 91.5 jit_solution(15876367672362824056)
XLA Ops:
  0.0 89.2 %shard_map.46 = f32[224,1024]{1,0:T(8,128)} custom-call(bf16[64,512]{1,0:T(8,128)(2,1)} %acts.1, bf16[224,512]{1,0:T(8,128)(2,1)} %grads.1, bf16[64,4096]{1,0:T(8,128)(2,1)} %basis_a.1, bf16[224,14336]{1,0:T(8,128)(2,1)} %basis_g.1), custom_call_target="tpu_custom_call" | custom-call | tf_op jit(solution)/shard_map/pallas_call | solution.py:384
  89.3 2.2 %copy.6 = f32[224,1024]{1,0:T(8,128)} copy(f32[224,1024]{1,0:T(8,128)} %shard_map.46) | data formatting | bytes 1835008

commit v4 on v3

--- a/solution.py
+++ b/solution.py
@@ -21,7 +21,7 @@
         return self.send.at[i], self.recv.at[i]
 
 
-N_COPIES = 144
+N_COPIES = 160
 N_LOCAL = 24
 
 THREE = (1, 3, 2)
@@ -33,23 +33,25 @@
 
 
 SCHEDULE = (
-    ("bx", 0, 0, 2), ("ax", 1), ("gz", 2), ("ax", 3), ("gf", 0), ("ax", 2), ("af", 0), ("af", 3), ("af", 1),
-    ("as", 3), ("af", 2), ("vz", 0), ("gs", 2), ("as", 2), ("bx", 0, 0, 1), ("gz", 1), ("bx", 0, 0, 3),
-    ("bx", 1, 0, 1), ("bs", 0, 0, 2), ("as", 1), ("pa",), ("bx", 1, 0, 3), ("gf", 2), ("gz", 3), ("bx", 0, 1, 1),
-    ("bx", 0, 1, 3), ("gs", 1), ("bs", 0, 0, 1), ("bx", 1, 1, 2), ("sa",), ("gs", 3), ("bx", 0, 1, 2),
-    ("bs", 0, 0, 3), ("bs", 0, 1, 3), ("sx",), ("bs", 0, 1, 1), ("vz", 3), ("vz", 1), ("bs", 0, 1, 2), ("gf", 3),
-    ("gf", 1), ("bx", 1, 0, 2), ("cg", 0, 0), ("vz", 2), ("sxf", 1), ("sxf", 0), ("bs", 1, 1, 2), ("bx", 1, 1, 3),
-    ("bs", 1, 0, 3), ("bs", 1, 0, 1), ("cg", 0, 1), ("ss", 3), ("bx", 1, 1, 1), ("cg", 0, 2), ("cg", 0, 3),
-    ("bs", 1, 0, 2), ("ss", 2), ("bs", 1, 1, 1), ("ss", 1), ("cg", 1, 0), ("sf", 3), ("cg", 1, 1), ("bs", 1, 1, 3),
-    ("cg", 1, 2), ("us", 2), ("sf", 0), ("us", 1), ("cg", 1, 3), ("us", 3), ("sq", 0), ("sf", 2), ("sf", 1),
-    ("uf", 1), ("uf", 2), ("sq", 1), ("uf", 3), ("uf", 0), ("tb", 0), ("fin", 0), ("tb", 1), ("fin", 1), ("fin", 2),
-    ("fin", 3),
+    ("gz", 3), ("bx", 2, 0, 2), ("bx", 2, 0, 3), ("bx", 1, 1, 1), ("bx", 0, 0, 1), ("bx", 0, 0, 3), ("ax", 2),
+    ("as", 1), ("as", 2), ("bs", 2, 0, 3), ("gz", 2), ("ax", 3), ("gf", 0), ("ax", 1), ("af", 2), ("af", 3),
+    ("af", 0), ("vz", 0), ("bs", 2, 0, 2), ("bx", 0, 1, 2), ("af", 1), ("as", 3), ("gs", 3), ("gz", 1),
+    ("bs", 0, 0, 1), ("bx", 1, 1, 3), ("gs", 2), ("bx", 1, 0, 3), ("bx", 0, 1, 1), ("bx", 2, 0, 1), ("pa",),
+    ("bx", 2, 1, 1), ("bx", 2, 1, 3), ("bs", 0, 1, 2), ("vz", 1), ("bs", 2, 0, 1), ("bx", 0, 1, 3), ("bx", 1, 0, 1),
+    ("bs", 1, 1, 3), ("cg", 2, 0), ("gs", 1), ("bx", 1, 1, 2), ("gf", 2), ("bx", 2, 1, 2), ("bs", 2, 1, 3),
+    ("bx", 1, 0, 2), ("bs", 0, 0, 3), ("sa",), ("gf", 3), ("gf", 1), ("bs", 0, 1, 3), ("vz", 3), ("sx",),
+    ("bs", 1, 1, 1), ("vz", 2), ("cg", 2, 1), ("bs", 1, 0, 3), ("bs", 1, 0, 2), ("bs", 1, 0, 1), ("cg", 1, 0),
+    ("bs", 2, 1, 1), ("bx", 0, 0, 2), ("bs", 1, 1, 2), ("bs", 2, 1, 2), ("ss", 3), ("cg", 1, 1), ("bs", 0, 1, 1),
+    ("ss", 1), ("us", 1), ("cg", 1, 2), ("sxf", 1), ("sf", 0), ("sxf", 0), ("cg", 2, 2), ("bs", 0, 0, 2),
+    ("cg", 2, 3), ("cg", 1, 3), ("cg", 0, 0), ("cg", 0, 1), ("ss", 2), ("cg", 0, 2), ("cg", 0, 3), ("sq", 2),
+    ("sf", 3), ("sq", 1), ("sf", 1), ("us", 3), ("sf", 2), ("tb", 2), ("uf", 1), ("us", 2), ("sq", 0), ("uf", 3),
+    ("tb", 1), ("uf", 0), ("uf", 2), ("tb", 0), ("fin", 0), ("fin", 1), ("fin", 2), ("fin", 3),
 )
 
 
 SPLIT = 3
-PARTS = (160, 64)
-FLIP = 32
+PARTS = (96, 80, 48)
+FLIP = 64
 
 
 def kernel(acts, grads, basis_a, basis_g, out, xa, ba, pa, ra, sa, sq, xg, bg, acc, ps, pr, sg,

time: 92.2 us -> 95.1 us (1.031); the launches traced: 91.5 us -> 93.4 us
  Pallas kernels: 89.2 us -> 91.2 us
    pallas_call x1, Pallas kernels: 89.2 us -> 91.2 us  [body(): pl.pallas_call(kernel, out_shape=jax.ShapeDtypeStruct((dg, n_out), F32),...]
where the time goes in v4:
time: 95.1 us; the launch traced here: 93.4 us
  Pallas kernels  91.2 us (96%)
  local copies, waits for them, and re-layouts  2.2 us (2%)
    pallas_call x1, Pallas kernels, body(): pl.pallas_call(kernel, out_shape=jax.ShapeDtypeStruct((dg, n_out), F32),...  91.2 us
    unnamed x1, local copies, waits for them, and re-layouts  2.2 us

profile of v4, /device:TPU:1, one launch (start us, length us, event | category | flops | bytes accessed | tf_op | source)
XLA Modules:
  0.0 93.4 jit_solution(4666577685165291477)
XLA Ops:
  0.0 91.2 %shard_map.46 = f32[224,1024]{1,0:T(8,128)} custom-call(bf16[64,512]{1,0:T(8,128)(2,1)} %acts.1, bf16[224,512]{1,0:T(8,128)(2,1)} %grads.1, bf16[64,4096]{1,0:T(8,128)(2,1)} %basis_a.1, bf16[224,14336]{1,0:T(8,128)(2,1)} %basis_g.1), custom_call_target="tpu_custom_call" | custom-call | tf_op jit(solution)/shard_map/pallas_call | solution.py:386
  91.2 2.2 %copy.6 = f32[224,1024]{1,0:T(8,128)} copy(f32[224,1024]{1,0:T(8,128)} %shard_map.46) | data formatting | bytes 1835008

commit v5 on v3

--- a/solution.py
+++ b/solution.py
@@ -21,7 +21,7 @@
         return self.send.at[i], self.recv.at[i]
 
 
-N_COPIES = 144
+N_COPIES = 160
 N_LOCAL = 24
 
 THREE = (1, 3, 2)
@@ -148,17 +148,17 @@
     parts = range(len(PARTS))
     main, rest = grads.at[0:dg - flip, :], grads.at[dg - flip:dg, :]
 
-    def lanes(q):
-        return pl.ds(pl.multiple_of(q * quarter, quarter), quarter)
+    def lanes(t):
+        return pl.ds(pl.multiple_of(t * quarter, quarter), quarter)
 
     def sq_block(t, xs, zs, q):
-        return sq.at[t, pl.ds(pl.multiple_of((xs * NZ + zs) * da, da), da), lanes(q)]
+        return sq.at[q, pl.ds(pl.multiple_of((xs * NZ + zs) * da, da), da), lanes(t)]
 
     def sq_chunk(xs, q, first=0, rows=NZ * da):
-        return sq.at[0:SPLIT, pl.ds(pl.multiple_of(xs * (NZ * da) + first, 128), rows), lanes(q)]
+        return sq.at[q, pl.ds(pl.multiple_of(xs * (NZ * da) + first, 128), rows), 0:SPLIT * quarter]
 
     def sq_rest(xs, q):
-        return sq.at[SPLIT:NT, pl.ds(pl.multiple_of(xs * (NZ * da), NZ * da), NZ * da), lanes(q)]
+        return sq.at[q, pl.ds(pl.multiple_of(xs * (NZ * da), NZ * da), NZ * da), SPLIT * quarter:NT * quarter]
 
     a_z = {d: Copy("a_z", xa_at(x, dn(zl, d))) for d in THREE}
     a_x = {(j, d): Copy("a_x", xa_at(dn(x, d), dn(zl, j))) for j in range(4) for d in SIDES}
@@ -188,7 +188,7 @@
     u_f = {j: Copy("u_f", sq_rest(up(x, 2), dn(y, j))) for j in range(4)}
 
     def sg_at(t, h):
-        return sg.at[t, rows_of(h), :]
+        return sg.at[:, rows_of(h), lanes(t)]
 
     t_far = [Copy("t_far", sg_at(far, h)) for h in parts]
     t_sib = [Copy("t_sib", sg_at(sib, h)) for h in parts]
@@ -344,7 +344,9 @@
         total = acc[part_rows(h, x), :]
         for d in range(NX - 1):
             total = total + pr[d, rows_of(h), :].astype(F32)
-        sg[tok, rows_of(h), :] = (total * total).astype(BF16)
+        square = (total * total).astype(BF16)
+        for q in range(NY):
+            sg[q, rows_of(h), lanes(tok)] = square[:, q * quarter:(q + 1) * quarter]
         t_far[h].start(sg_at(tok, h), sg_at(tok, h), dev(tok=far))
         t_sib[h].start(sg_at(tok, h), sg_at(tok, h), dev(tok=sib))
 
@@ -352,16 +354,16 @@
         t_far[h].arrived()
         t_both[h].start(sg_at(far, h), sg_at(far, h), dev(tok=sib))
 
-    tile = 256
-    scale = 1.0 / (cols * NT)
-
     def fin(i):
         all_of(*((s_x, s_xf, s_y, s_f, u_y, u_x, u_f), (t_sib,), (t_far,), (t_both,))[i])
-        t = (tok, sib, far, up(sib, 2))[i]
+        if i < 3:
+            return
+        left = jnp.concatenate([sg[q] for q in range(NY)], axis=1)
+        tile = 256
         for n in range(0, out.shape[1], tile):
-            part = lax.dot_general(sg[t], sq[t, n:n + tile, :], (((1,), (1,)), ((), ())), preferred_element_type=F32)
-            value = part if i == 0 else out[:, n:n + tile] + part
-            out[:, n:n + tile] = value * scale if i == 3 else value
+            right = jnp.concatenate([sq[q, n:n + tile, :] for q in range(NY)], axis=1)
+            value = lax.dot_general(left, right, (((1,), (1,)), ((), ())), preferred_element_type=F32)
+            out[:, n:n + tile] = value * (1.0 / (cols * NT))
 
     steps = {"ax": ax, "af": af, "as": share_a, "pa": project_a, "sa": square_a, "sx": sx, "sxf": sxf, "ss": ss, "sf": sf,
              "us": us, "uf": uf, "gz": gz, "gs": gs, "gf": gf, "vz": vz, "bx": bx, "bs": bs, "cg": cg, "sq": square_g, "tb": tb,
@@ -392,13 +394,13 @@
             pltpu.VMEM((NY, rows_a, quarter), F32),
             pltpu.VMEM((NY - 1, rows_a, quarter), F32),
             pltpu.VMEM((rows_a, quarter), BF16),
-            pltpu.VMEM((NT, n_out, cols), BF16),
+            pltpu.VMEM((NY, n_out, NT * quarter), BF16),
             pltpu.VMEM((NY, fx, cols), BF16),
             pltpu.VMEM((NY, NX * dg, fx), BF16),
             pltpu.VMEM((NX * dg, cols), F32),
             pltpu.VMEM((NX * dg, cols), BF16),
             pltpu.VMEM((NX - 1, dg, cols), BF16),
-            pltpu.VMEM((NT, dg, cols), BF16),
+            pltpu.VMEM((NY, dg, NT * quarter), BF16),
             pltpu.SemaphoreType.DMA((N_COPIES,)),
             pltpu.SemaphoreType.DMA((N_COPIES,)),
             pltpu.SemaphoreType.DMA((N_LOCAL,)),

time: 92.2 us -> 93.3 us (1.012)
  Pallas kernels: 89.2 us -> 90.4 us
    pallas_call x1, Pallas kernels: 89.2 us -> 90.4 us  [body(): pl.pallas_call(kernel, out_shape=jax.ShapeDtypeStruct((dg, n_out), F32),...]
where the time goes in v5:
time: 93.3 us; the launch traced here: 92.6 us
  Pallas kernels  90.4 us (97%)
  local copies, waits for them, and re-layouts  2.2 us (2%)
    pallas_call x1, Pallas kernels, body(): pl.pallas_call(kernel, out_shape=jax.ShapeDtypeStruct((dg, n_out), F32),...  90.4 us
    unnamed x1, local copies, waits for them, and re-layouts  2.2 us

profile of v5, /device:TPU:1, one launch (start us, length us, event | category | flops | bytes accessed | tf_op | source)
XLA Modules:
  0.0 92.6 jit_solution(13153645430372260714)
XLA Ops:
  0.0 90.4 %shard_map.46 = f32[224,1024]{1,0:T(8,128)} custom-call(bf16[64,512]{1,0:T(8,128)(2,1)} %acts.1, bf16[224,512]{1,0:T(8,128)(2,1)} %grads.1, bf16[64,4096]{1,0:T(8,128)(2,1)} %basis_a.1, bf16[224,14336]{1,0:T(8,128)(2,1)} %basis_g.1), custom_call_target="tpu_custom_call" | custom-call | tf_op jit(solution)/shard_map/pallas_call | solution.py:386
  90.4 2.2 %copy.6 = f32[224,1024]{1,0:T(8,128)} copy(f32[224,1024]{1,0:T(8,128)} %shard_map.46) | data formatting | bytes 1835008

commit v6 on v3

--- a/solution.py
+++ b/solution.py
@@ -100,7 +100,7 @@
             cp = pltpu.make_async_remote_copy(src_ref=src, dst_ref=dst, send_sem=s, recv_sem=r,
                                               device_id=to, device_id_type=MESH)
             cp.start()
-            sent.append(cp)
+            sent.append((self.tag, cp))
 
         def arrived(self):
             if self.here:
@@ -355,7 +355,14 @@
     tile = 256
     scale = 1.0 / (cols * NT)
 
+    def settle(recent):
+        for tag, cp in [one for one in sent if one[0] not in recent]:
+            cp.wait_send()
+            sent.remove((tag, cp))
+
     def fin(i):
+        if i == 0:
+            settle(("s_y", "s_f", "u_x", "u_f", "t_far", "t_sib", "t_both"))
         all_of(*((s_x, s_xf, s_y, s_f, u_y, u_x, u_f), (t_sib,), (t_far,), (t_both,))[i])
         t = (tok, sib, far, up(sib, 2))[i]
         for n in range(0, out.shape[1], tile):
@@ -369,8 +376,7 @@
     for name, *where in SCHEDULE:
         steps[name](*where)
 
-    for cp in sent:
-        cp.wait_send()
+    settle(())
 
 
 def body(acts_t, grads_t, basis_a, basis_g):

time: 92.2 us -> 92 us (level)
  no operation moved by 1% of the time
where the time goes in v6:
time: 92 us; the launch traced here: 91.3 us
  Pallas kernels  89.1 us (97%)
  local copies, waits for them, and re-layouts  2.2 us (2%)
    pallas_call x1, Pallas kernels, body(): pl.pallas_call(kernel, out_shape=jax.ShapeDtypeStruct((dg, n_out), F32),...  89.1 us
    unnamed x1, local copies, waits for them, and re-layouts  2.2 us

profile of v6, /device:TPU:1, one launch (start us, length us, event | category | flops | bytes accessed | tf_op | source)
XLA Modules:
  0.0 91.3 jit_solution(10818253379411537403)
XLA Ops:
  0.0 89.1 %shard_map.46 = f32[224,1024]{1,0:T(8,128)} custom-call(bf16[64,512]{1,0:T(8,128)(2,1)} %acts.1, bf16[224,512]{1,0:T(8,128)(2,1)} %grads.1, bf16[64,4096]{1,0:T(8,128)(2,1)} %basis_a.1, bf16[224,14336]{1,0:T(8,128)(2,1)} %basis_g.1), custom_call_target="tpu_custom_call" | custom-call | tf_op jit(solution)/shard_map/pallas_call | solution.py:390
  89.1 2.2 %copy.6 = f32[224,1024]{1,0:T(8,128)} copy(f32[224,1024]{1,0:T(8,128)} %shard_map.46) | data formatting | bytes 1835008

commit v7 on v6

--- a/solution.py
+++ b/solution.py
@@ -48,7 +48,7 @@
 
 
 SPLIT = 3
-PARTS = (160, 64)
+PARTS = (144, 80)
 FLIP = 32
 
 

time: 92 us -> 92 us (level)
  no operation moved by 1% of the time
where the time goes in v7:
time: 92 us; the launch traced here: 91.9 us
  Pallas kernels  89.7 us (98%)
  local copies, waits for them, and re-layouts  2.2 us (2%)
    pallas_call x1, Pallas kernels, body(): pl.pallas_call(kernel, out_shape=jax.ShapeDtypeStruct((dg, n_out), F32),...  89.7 us
    unnamed x1, local copies, waits for them, and re-layouts  2.2 us

profile of v7, /device:TPU:1, one launch (start us, length us, event | category | flops | bytes accessed | tf_op | source)
XLA Modules:
  0.0 91.9 jit_solution(2796984474516318020)
XLA Ops:
  0.0 89.7 %shard_map.46 = f32[224,1024]{1,0:T(8,128)} custom-call(bf16[64,512]{1,0:T(8,128)(2,1)} %acts.1, bf16[224,512]{1,0:T(8,128)(2,1)} %grads.1, bf16[64,4096]{1,0:T(8,128)(2,1)} %basis_a.1, bf16[224,14336]{1,0:T(8,128)(2,1)} %basis_g.1), custom_call_target="tpu_custom_call" | custom-call | tf_op jit(solution)/shard_map/pallas_call | solution.py:390
  89.7 2.2 %copy.6 = f32[224,1024]{1,0:T(8,128)} copy(f32[224,1024]{1,0:T(8,128)} %shard_map.46) | data formatting | bytes 1835008
